TPU v7x, 32 devices: a whole 2x2x4 slice. The times are simulated.
32 devices in a mesh: dp: 8 (over y, x, core), mp: 4 (over z).
Axes of the slice: x: 2, y: 2, z: 4, core: 2. Of those that a mesh axis runs over, the one named last changes fastest.
Arguments:
- ids: int32 [32768], P('dp'), may hold values from 0 to 32767
- hash_mult: int32 [1024], replicated, may hold values from 1 to 65520
- hash_add: int32 [1024], replicated, may hold values from 0 to 65520
- weight_first: bfloat16 [1800, 1024], P('mp'), may hold values from -0.1875 to 0.1875
- bias_first: float32 [1800], P('mp'), may hold values from -4 to 4
- scale_first: float32 [1800], P('mp'), may hold values from 0.1 to 1.9
- shift_first: float32 [1800], P('mp'), may hold values from -3 to 3
- weight_second: bfloat16 [1800, 1800], P('mp'), may hold values from -0.125 to 0.125
- bias_second: float32 [1800], P('mp'), may hold values from -4 to 4
- scale_second: float32 [1800], P('mp'), may hold values from 0.1 to 1.9
- shift_second: float32 [1800], P('mp'), may hold values from -3 to 3
- cotangent: bfloat16 [1800, 32768], P('mp', 'dp'), may hold values from -6 to 6
Outputs:
- output: bfloat16 [1800, 32768], P('mp', 'dp')
- grad_weight_first: float32 [1800, 1024], P('mp')
- grad_bias_first: float32 [1800], P('mp')
- grad_scale_first: float32 [1800], P('mp')
- grad_shift_first: float32 [1800], P('mp')
- grad_weight_second: float32 [1800, 1800], P('mp')
- grad_bias_second: float32 [1800], P('mp')
- grad_scale_second: float32 [1800], P('mp')
- grad_shift_second: float32 [1800], P('mp')
All inputs are finite; a program needn't handle non-finite values.
Results may differ from a plain program's by a relative error of at most 0.03.
Values may be sent and summed in bfloat16 or wider, within the bound.
A program may use at most 192 MiB of HBM per device.

v0:
```python
import functools

import jax
import jax.numpy as jnp
from jax import lax
from jax.experimental import pallas as pl
from jax.experimental.pallas import tpu as pltpu
from jax.sharding import PartitionSpec as P

MESH = pl.DeviceIdType.MESH
F32, BF16, I32 = jnp.float32, jnp.bfloat16, jnp.int32
epsilon = 1e-05


def dot(a, b):
    return lax.dot_general(a, b, (((1,), (0,)), ((), ())), preferred_element_type=F32)


def dot_nt(a, b):
    return lax.dot_general(a, b, (((1,), (1,)), ((), ())), preferred_element_type=F32)


def mish_parts(v):
    u = jnp.exp(jnp.minimum(v, 20.0))
    n = u * (u + 2.0)
    d = n + 2.0
    r = pl.reciprocal(d, approx=True)
    t = n * r
    return v * t, t + v * ((4.0 * (n - u) * r) * r)


def mish(v):
    u = jnp.exp(jnp.minimum(v, 20.0))
    n = u * (u + 2.0)
    d = n + 2.0
    r = pl.reciprocal(d, approx=True)
    return v * (n * r)


def lane_part(x):
    out = x[:, :128]
    for at in range(128, x.shape[1], 128):
        out = out + x[:, at : at + 128]
    return out


def kernel(
    D, M, U, LP, K, R,
    ids_ref, mult_ref, add_ref, par_ref, w1_ref, w2_ref, cot_ref,
    out_ref, gw1_ref, gw2_ref, vec_ref,
    A, B, C, W2, G1, E1, F, H, act2, slo2, col, RW, acc, hcol,
    pv, ar1, ar2, ar2z, ar3, ar3z, ar4, ar4s, ar4z,
    w1s, w1r, w2s, w2r, pvs, pvr, cts, ctr, loc,
    a1s, a1r, a2s, a2r, a2zs, a2zr, a3s, a3r, a3zs, a3zr, a4s, a4r, a4zs, a4zr,
    g1s, g1r, g2s, g2r, free, *extra,
):
    Q = R // M
    G = D // 8
    TL = min(512, Q)
    NT = Q // TL
    PER = K // LP
    NA = M // PER
    K8 = K // 8
    J8 = M * LP // 8
    S8 = LP // 8
    N = float(R * D)
    d = lax.axis_index("dp")
    m = lax.axis_index("mp")
    i = lax.rem(d, 8)
    c = lax.rem(i, 2)
    x = lax.rem(i // 2, 2)
    y = i // 4
    hi = (1 - c) * x + c * y
    lo = (1 - c) * y + c * x
    p = 4 * c + 2 * hi + lo
    core_dev = (d + 1 - 2 * c, m)
    flip_x = d + 2 - 4 * x
    flip_y = d + 4 - 8 * y
    hi_dev = ((1 - c) * flip_x + c * flip_y, m)
    lo_dev = ((1 - c) * flip_y + c * flip_x, m)
    up = [lax.rem(m + k, M) for k in range(M)]
    down = [lax.rem(m - k + M, M) for k in range(M)]
    others = [lax.rem(d + k, D) for k in range(D)]
    sent = []

    def remote(src, dst, ss, rs, dev):
        cp = pltpu.make_async_remote_copy(
            src_ref=src, dst_ref=dst, send_sem=ss, recv_sem=rs, device_id=dev, device_id_type=MESH
        )
        return cp

    def send(src, dst, ss, rs, dev):
        cp = remote(src, dst, ss, rs, dev)
        cp.start()
        sent.append(cp)
        return cp

    def gone(cp):
        cp.wait_send()
        sent[:] = [other for other in sent if other is not cp]

    def lanes(ref, at, size):
        return ref.at[:, pl.ds(pl.multiple_of(at, 128), size)]

    def rows(ref, at, size):
        return ref.at[pl.ds(pl.multiple_of(at, 16), size)]

    bar = pltpu.get_barrier_semaphore()
    greeted = [core_dev, hi_dev, lo_dev] if G == 1 else [(others[k], m) for k in range(1, D)]
    greeted += [(d, up[k]) for k in range(1, M)]
    for dev in greeted:
        pl.semaphore_signal(bar, inc=1, device_id=dev, device_id_type=MESH)

    w2_loc = pltpu.make_async_copy(w2_ref, G1, loc.at[1])
    w2_loc.start()
    w1_loc = pltpu.make_async_copy(w1_ref, C.at[m], loc.at[0])
    w1_loc.start()
    cot_loc = pltpu.make_async_copy(lanes(cot_ref, m * Q, Q), lanes(F.at[m], 0, Q), loc.at[2])
    pv[m] = par_ref[...]
    pl.semaphore_wait(bar, len(greeted))

    ag1, ag2, agp, ct = {}, {}, {}, {}
    for k in range(1, M):
        agp[k] = send(par_ref, pv.at[m], pvs.at[k], pvr.at[k], (d, up[k]))
    for ag, own, buf, size, ss, rs in ((ag1, w1_ref, C, K8, w1s, w1r), (ag2, None, W2, J8, w2s, w2r)):
        for k in range(1, M):
            part = lanes(buf.at[m], p * size, size)
            mine = part if own is None else lanes(own, p * size, size)
            ag[0, k] = remote(mine, part, ss.at[0, k], rs.at[0, k], (d, up[k]))
            for step, dev, at, width in (
                (1, lo_dev, p, 1), (2, hi_dev, 4 * c + 2 * hi, 2), (3, core_dev, 4 * c, 4)
            ):
                part = lanes(buf.at[down[k]], at * size, width * size)
                ag[step, k] = remote(part, part, ss.at[step, k], rs.at[step, k], dev)
    for k in range(1, M):
        ag1[0, k].start()
    w2_loc.wait()
    for b in range(M):
        W2[m, :, (b + 1) * LP - 128 : (b + 1) * LP] = jnp.zeros((U, 128), BF16)
        W2[m, :, b * LP : b * LP + U] = G1[:, b * U : (b + 1) * U]

    def gather_stage(step, ag):
        for k in range(1, M):
            ag[step - 1, k].wait_recv()
            ag[step, k].start()

    def stage1(step):
        gather_stage(step, ag1)

    def stage2(step):
        gather_stage(step, ag2)

    hrow = jnp.concatenate(
        [mult_ref[...].astype(F32), add_ref[...].astype(F32), jnp.zeros((126, K), F32)], axis=0
    )
    hcol[...] = hrow.T

    HT = 128

    def encode(q, put):
        def step(t, _):
            at = pl.multiple_of(t * HT, HT)
            both = hcol[pl.ds(at, HT), :].astype(I32)
            v = both[:, 0:1] * ids_ref[:, pl.ds(pl.multiple_of(q * Q, 128), Q)] + both[:, 1:2]
            for _ in range(2):
                top = lax.shift_right_logical(v, 16)
                v = (v & 65535) + ((top << 4) - top)
            v = jnp.where(v >= 65521, v - 65521, v)
            put(t, (v.astype(F32) * (2.0 / 65520.0) - 1.0).astype(BF16))
            return 0

        lax.fori_loop(0, K // HT, step, 0)

    def make_col(b):
        col[b] = jnp.concatenate([RW[b], jnp.zeros((128 - RW.shape[1], LP), F32)], axis=0).T

    def make_cols():
        def step(b, _):
            make_col(b)
            return 0

        lax.fori_loop(0, M, step, 0)

    def to_a(q):
        def put(t, value):
            A[q, pl.ds(pl.multiple_of(t * HT, HT), HT), :] = value

        return put

    def to_e1(t, value):
        E1[pl.ds(pl.multiple_of(lax.rem(t, LP // HT) * HT, HT), HT), pl.ds(pl.multiple_of(t // (LP // HT) * Q, 128), Q)] = value

    def row_of(slot):
        return jnp.sum(acc[slot].T, axis=0, keepdims=True)

    acc[...] = jnp.zeros_like(acc)
    for b in range(M):
        B[pl.ds(b * LP + U // 16 * 16, LP - U // 16 * 16), :] = jnp.zeros((LP - U // 16 * 16, R), BF16)

    RW[...] = jnp.zeros_like(RW)
    RW[m, 0:8] = par_ref[...]
    make_col(m)
    encode(m, to_a(m))
    w1_loc.wait()

    def mm1_own(b):
        def step(t, _):
            at = pl.multiple_of(t * TL, TL)
            act, slope = mish_parts(dot(C[b], A[m, :, pl.ds(at, TL)]) + col[b, :U, 0:1])
            H[b, :, pl.ds(at, TL)] = slope.astype(BF16)
            B[pl.ds(pl.multiple_of(b * LP, LP), U), pl.ds(pl.multiple_of(m * Q + t * TL, TL), TL)] = act.astype(BF16)
            acc[0, :U] += lane_part(act)
            acc[1, :U] += lane_part(act * act)
            return 0

        lax.fori_loop(0, NT, step, 0)

    def mm1_rest(b):
        def step(t, _):
            q = lax.rem(m + t, M)
            act = mish(dot(C[b], A[q]) + col[b, :U, 0:1])
            B[pl.ds(pl.multiple_of(b * LP, LP), U), pl.ds(pl.multiple_of(q * Q, Q), Q)] = act.astype(BF16)
            acc[0, :U] += lane_part(act)
            acc[1, :U] += lane_part(act * act)
            return 0

        lax.fori_loop(1, M, step, 0)

    def mm1_sums(b):
        ar1[d, pl.ds(b, 1), :] = row_of(0)
        ar1[d, pl.ds(b + M, 1), :] = row_of(1)
        acc[0:2] = jnp.zeros((2, LP, 128), F32)

    mm1_own(m)
    stage1(1)
    for k in range(1, M):
        ag2[0, k].start()

    def enc_step(k, _):
        q = lax.rem(m + M - k, M)
        encode(q, to_a(q))
        return 0

    lax.fori_loop(1, M, enc_step, 0)
    stage1(2)
    mm1_rest(m)
    mm1_sums(m)
    stage2(1)
    cot_loc.start()
    for q in range(1, M):
        ct[q] = send(
            lanes(cot_ref, up[q] * Q, Q), lanes(F.at[m], 0, Q), cts.at[q], ctr.at[q], (d, up[q])
        )
    stage1(3)
    for k in range(1, M):
        agp[k].wait_recv()
    for b in range(M):
        RW[b, 0:8] = pv[b]
    make_cols()
    def mm1_other(k, _):
        b = lax.rem(m + M - k, M)
        part = lanes(C.at[b], 4 * c * K8, 4 * K8)
        remote(part, part, w1s.at[3, k], w1r.at[3, k], core_dev).wait_recv()
        mm1_own(b)
        mm1_rest(b)
        mm1_sums(b)
        pl.when(k == 1)(functools.partial(stage2, 2))
        return 0

    lax.fori_loop(1, M, mm1_other, 0)

    def all_dp(buf, ss, rs):
        cps = []
        for k in range(1, D):
            cps.append(send(buf.at[d], buf.at[d], ss.at[k], rs.at[k], (others[k], m)))
        return cps

    def total(buf, cps):
        for cp in cps:
            cp.wait_recv()
        out = buf[0]
        for k in range(1, D):
            out = out + buf[k]
        return out

    cps1 = all_dp(ar1, a1s, a1r)
    stage2(3)
    for cp in ag1.values():
        cp.wait_send()
    cot_all = []
    for q in range(M):
        cp = pltpu.make_async_copy(lanes(cot_ref, q * Q, Q), lanes(C.at[q], 0, Q), loc.at[3 + q])
        cot_all.append(cp)
        cp.start()
    for k in range(1, M):
        ag2[3, k].wait_recv()

    def make_e1(b):
        def step(h, _):
            part = W2[h, :, pl.ds(pl.multiple_of(b * LP, LP), LP)].astype(F32) * col[h, :U, 1:2]
            for n in range(LP // 128):
                acc[n, :U] = part[:, n * 128 : (n + 1) * 128]
            for n in range(LP // 128):
                E1[n * 128 : (n + 1) * 128, pl.ds(pl.multiple_of(h * LP, LP), LP)] = acc[n].T.astype(BF16)
            return 0

        lax.fori_loop(0, M, step, 0)
        acc[...] = jnp.zeros_like(acc)

    const = jnp.zeros((8, M * LP), F32)
    for b in range(M):
        shift = jnp.broadcast_to(pv[b, 2:3, :U], (8, U))
        upper = shift.astype(BF16)
        lower = (shift - upper.astype(F32)).astype(BF16)
        const = const + dot(upper, W2[b]) + dot(lower, W2[b])
    for b in range(M):
        RW[b, 8:9] = const[0:1, b * LP : (b + 1) * LP] + pv[b, 3:4]
    make_e1(m)

    tot = total(ar1, cps1)
    mean = tot[:M] / N
    inv = lax.rsqrt(tot[M:] / N - mean * mean + epsilon)
    for b in range(M):
        RW[b, 9:10] = inv[b : b + 1]
        RW[b, 10:11] = -mean[b : b + 1] * inv[b : b + 1]
    make_cols()
    for cp in cot_all:
        cp.wait()

    def mm2(t, _):
        at = pl.multiple_of(t * TL, TL)
        for b in range(M):
            part = B[b * LP : b * LP + U, pl.ds(at, TL)].astype(F32)
            B[b * LP : b * LP + U, pl.ds(at, TL)] = (part * col[b, :U, 9:10] + col[b, :U, 10:11]).astype(BF16)
        v = dot(E1[:U], B[:, pl.ds(at, TL)]) + col[m, :U, 8:9]
        act, slope = mish_parts(v)
        act2[:, pl.ds(at, TL)] = act.astype(BF16)
        slo2[:, pl.ds(at, TL)] = slope.astype(BF16)
        g = C[t // NT, :, pl.ds(pl.multiple_of(lax.rem(t, NT) * TL, TL), TL)].astype(F32)
        acc[0, :U] += lane_part(act)
        acc[1, :U] += lane_part(act * act)
        acc[2, :U] += lane_part(g)
        acc[3, :U] += lane_part(g * act)
        return 0

    lax.fori_loop(0, M * NT, mm2, 0)
    for s in range(4):
        ar2[d, s : s + 1, :] = row_of(s)
    ar2[d, 4:8, :] = jnp.zeros((4, LP), F32)
    acc[...] = jnp.zeros_like(acc)
    cps2 = all_dp(ar2, a2s, a2r)

    def a_at(base, b):
        return base + b // PER, pl.multiple_of(lax.rem(b, PER) * LP, LP)

    def mm2_own(b):
        make_e1(b)
        act_at, row = a_at(0, b)
        v = dot(E1[:U], B[:, pl.ds(pl.multiple_of(m * Q, Q), Q)]) + col[b, :U, 8:9]
        act, slope = mish_parts(v)
        A[act_at, pl.ds(row, U)] = act.astype(BF16)
        A[act_at + NA, pl.ds(row, U)] = slope.astype(BF16)

    def own_loop(k, _):
        mm2_own(lax.rem(m + k, M))
        return 0

    mm2_own(up[1])
    tot = total(ar2, cps2)
    mean = tot[0:1] / N
    inv = lax.rsqrt(tot[1:2] / N - mean * mean + epsilon)
    sum_g = tot[2:3]
    sum_gn = inv * (tot[3:4] - mean * sum_g)
    k1 = pv[m, 4:5] * inv
    k2 = -k1 * inv * sum_gn / N
    k3 = -k1 * sum_g / N - mean * k2
    ar2z[m, 0:1] = k1
    ar2z[m, 1:2] = k2
    ar2z[m, 2:3] = k3
    ar2z[m, 3:4] = k1
    ar2z[m, 4:5] = pv[m, 5:6] - mean * k1
    ar2z[m, 5:6] = sum_g
    ar2z[m, 6:7] = sum_gn
    ar2z[m, 7:8] = jnp.zeros((1, LP), F32)
    cps2z = [send(ar2z.at[m], ar2z.at[m], a2zs.at[k], a2zr.at[k], (d, up[k])) for k in range(1, M)]
    RW[m, 16:24] = ar2z[m]
    make_col(m)

    def back2(t, _):
        at = pl.multiple_of(t * TL, TL)
        a = act2[:, pl.ds(at, TL)].astype(F32)
        g = C[t // NT, :, pl.ds(pl.multiple_of(lax.rem(t, NT) * TL, TL), TL)].astype(F32)
        grad = (g * col[m, :U, 16:17] + a * col[m, :U, 17:18] + col[m, :U, 18:19]) * slo2[:, pl.ds(at, TL)].astype(F32)
        grad = grad.astype(BF16)
        slo2[:, pl.ds(at, TL)] = grad
        acc[0, :U] += lane_part(grad.astype(F32))
        return 0

    lax.fori_loop(0, M * NT, back2, 0)
    gb2 = row_of(0)
    ar3[d, 2 * M : 2 * M + 1, :] = gb2
    ar3[d, 2 * M + 1 : 2 * M + 8, :] = jnp.zeros((7, LP), F32)
    acc[0:1] = jnp.zeros((1, LP, 128), F32)

    L1 = pl.multiple_of(lax.rem(m + 1, M) * Q, 128)
    LR = pl.multiple_of(L1 + LP, 128)

    def rowsum(x):
        acc[0, :U] = lane_part(x[:, : U // 128 * 128]) + jnp.where(
            lax.broadcasted_iota(I32, (U, 128), 1) >= 128 - U % 128, x[:, U - 128 :], 0.0
        )
        return row_of(0)

    gb2_all8 = jnp.broadcast_to(gb2[:, :U], (8, U))
    gb2_up = gb2_all8.astype(BF16)
    gb2_low = (gb2_all8 - gb2_up.astype(F32)).astype(BF16)
    ar3[d, 0 : 2 * M, :] = jnp.zeros((2 * M, LP), F32)

    def grad_w2(b, _):
        at = pl.multiple_of(b * LP, LP)
        g = dot_nt(B[pl.ds(at, LP), :], slo2[...])
        w16 = W2[b, :, pl.ds(pl.multiple_of(m * LP, LP), LP)][:, :U]
        w = w16.astype(F32)
        ar3[d, pl.ds(b, 1), :U] = dot_nt(gb2_up, w16)[0:1] + dot_nt(gb2_low, w16)[0:1]
        ar3[d, pl.ds(b + M, 1), :] = rowsum(w * g[:U])
        g = g * col[b, :, 1:2] + col[b, :, 2:3] * gb2[:, :U]
        B[pl.ds(at, LP), pl.ds(L1, U)] = g.astype(BF16)
        B[pl.ds(at, LP), pl.ds(L1 + U // 128 * 128, LP - U // 128 * 128)] = jnp.where(
            lax.broadcasted_iota(I32, (LP, LP - U // 128 * 128), 1) < U - U // 128 * 128,
            B[pl.ds(at, LP), pl.ds(L1 + U // 128 * 128, LP - U // 128 * 128)].astype(F32),
            0.0,
        ).astype(BF16)
        return 0

    lax.fori_loop(0, M, grad_w2, 0)
    cps3 = all_dp(ar3, a3s, a3r)
    for n, dev in ((0, core_dev), (1, hi_dev), (2, lo_dev)):
        pl.semaphore_signal(free.at[n], inc=1, device_id=dev, device_id_type=MESH)
    for k in range(1, M):
        pl.semaphore_signal(free.at[2 + k], inc=1, device_id=(d, up[k]), device_id_type=MESH)

    HALF = {0: (1 - c) * 4, 1: 4 * c + 2 * (1 - hi), 2: 4 * c + 2 * hi + 1 - lo}
    KEEP = {0: 4 * c, 1: 4 * c + 2 * hi, 2: p}
    START = {0: 0, 1: 4, 2: 6}
    PARTNER = {0: core_dev, 1: hi_dev, 2: lo_dev}
    g2cp = {}

    def b_rows(b, at, size, lane):
        return B.at[pl.ds(pl.multiple_of(b * LP + at * S8, 16), size * S8), pl.ds(lane, LP)]

    def g2_send(n):
        pl.semaphore_wait(free.at[n], 1)
        for b in range(M):
            g2cp[n, b].start()

    def g2_add(n):
        for b in range(M):
            g2cp[n, b].wait_recv()
            size = (4 >> n) * S8
            keep = pl.ds(pl.multiple_of(b * LP + KEEP[n] * S8, 16), size)
            came = pl.ds(b * LP + START[n] * S8, size)
            B[keep, pl.ds(L1, LP)] = (
                B[keep, pl.ds(L1, LP)].astype(F32) + B[came, pl.ds(LR, LP)].astype(F32)
            ).astype(BF16)

    def l2_of(z):
        return pl.multiple_of(lax.rem(z + 2, M) * Q, 128)

    L2 = l2_of(m)
    for b in range(M):
        for n in range(3):
            g2cp[n, b] = remote(
                b_rows(b, HALF[n], 4 >> n, L1), b_rows(b, START[n], 4 >> n, LR), g2s.at[n, b], g2r.at[n, b], PARTNER[n]
            )
        for n, at, size, dev in ((4, p, 1, lo_dev), (5, 4 * c + 2 * hi, 2, hi_dev), (6, 4 * c, 4, core_dev)):
            part = b_rows(b, at, size, L2)
            g2cp[n, b] = remote(part, part, g2s.at[n, b], g2r.at[n, b], dev)
        if b:
            g2cp[3, b] = remote(
                b_rows(up[b], p, 1, L1),
                B.at[pl.ds(pl.multiple_of(m * LP + p * S8, 16), S8), pl.ds(l2_of(up[b]), LP)],
                g2s.at[3, b], g2r.at[3, b], (d, up[b]),
            )

    if G > 1:
        x1, x2, x1s, x1r, x2s, x2r = extra

    def g2_groups():
        cps = []
        for k in range(1, G):
            to = (lax.rem(d + 8 * k, D), m)
            for b in range(M):
                cps.append(send(b_rows(b, p, 1, L1), x2.at[d // 8, b], x2s.at[k, b], x2r.at[k, b], to))
        for b in range(M):
            x2[d // 8, b] = B[pl.ds(pl.multiple_of(b * LP + p * S8, 16), S8), pl.ds(L1, LP)]
        for cp in cps:
            cp.wait_recv()
        for cp in cps:
            gone(cp)
        for b in range(M):
            v = x2[0, b].astype(F32)
            for k in range(1, G):
                v = v + x2[k, b].astype(F32)
            B[pl.ds(pl.multiple_of(b * LP + p * S8, 16), S8), pl.ds(L1, LP)] = v.astype(BF16)

    def g2_z():
        if G > 1:
            g2_groups()
        for k in range(1, M):
            pl.semaphore_wait(free.at[2 + M - k], 1)
            g2cp[3, k].start()
        mine = pl.ds(pl.multiple_of(m * LP + p * S8, 16), S8)
        B[mine, pl.ds(L2, LP)] = B[mine, pl.ds(L1, LP)]

    def g2_gather(n):
        for b in range(1 if n == 4 else 0, M):
            g2cp[n - 1, b].wait_recv()
        for b in range(M):
            g2cp[n, b].start()

    g2_send(0)
    lax.fori_loop(2, M, own_loop, 0)
    tot = total(ar3, cps3)
    ar3z[m] = tot[: 2 * M]
    gb2_all = tot[2 * M : 2 * M + 1]
    cps3z = [send(ar3z.at[m], ar3z.at[m], a3zs.at[k], a3zr.at[k], (d, up[k])) for k in range(1, M)]
    g2_add(0)
    g2_send(1)
    encode(m, to_e1)
    for cp in cps2z:
        cp.wait_recv()
    for b in range(M):
        RW[b, 16:24] = ar2z[b]
    for cp in cps3z:
        cp.wait_recv()
    tot = ar3z[0]
    for b in range(1, M):
        tot = tot + ar3z[b]
    for b in range(M):
        k1 = pv[b, 1:2] * RW[b, 9:10]
        RW[b, 24:25] = k1
        RW[b, 25:26] = -k1 * tot[M + b : M + b + 1] / N
        RW[b, 26:27] = -k1 * tot[b : b + 1] / N
    make_cols()
    pick = lax.broadcasted_iota(I32, (2 * M, 1), 0)
    vec_ref[0:1, :] = jnp.zeros((1, LP), F32)
    vec_ref[1:2, :] = jnp.sum(jnp.where(pick == M + m, tot, 0.0), axis=0, keepdims=True)
    vec_ref[2:3, :] = jnp.sum(jnp.where(pick == m, tot, 0.0), axis=0, keepdims=True)
    vec_ref[3:4, :] = gb2_all
    vec_ref[4:5, :] = ar2z[m, 6:7]
    vec_ref[5:6, :] = ar2z[m, 5:6]
    vec_ref[6:8, :] = jnp.zeros((2, LP), F32)

    PADAT = U // 16 * 16

    def put_grad(b, value, at, size):
        slot, row = a_at(NA, b)
        A[slot, pl.ds(row, U), pl.ds(at, size)] = value

    for b in range(M):
        slot, row = NA + b // PER, (b % PER) * LP
        A[slot, row + PADAT : row + LP, :] = jnp.where(
            lax.broadcasted_iota(I32, (LP - PADAT, Q), 0) < U - PADAT,
            A[slot, row + PADAT : row + LP, :].astype(F32),
            0.0,
        ).astype(BF16)
    cot_loc.wait()

    def back2_own(b):
        act_at, row = a_at(0, b)

        def step(t, _):
            at = pl.multiple_of(t * TL, TL)
            a = A[act_at, pl.ds(row, U), pl.ds(at, TL)].astype(F32)
            s = A[act_at + NA, pl.ds(row, U), pl.ds(at, TL)].astype(F32)
            g = F[b, :, pl.ds(at, TL)].astype(F32)
            grad = (g * col[b, :U, 16:17] + a * col[b, :U, 17:18] + col[b, :U, 18:19]) * s
            A[act_at + NA, pl.ds(row, U), pl.ds(at, TL)] = grad.astype(BF16)
            return 0

        lax.fori_loop(0, NT, step, 0)

    def copy_own(t, _):
        at = pl.multiple_of(t * TL, TL)
        put_grad(m, slo2[:, pl.ds(pl.multiple_of(m * Q + t * TL, TL), TL)], at, TL)
        return 0

    lax.fori_loop(0, NT, copy_own, 0)
    for k in range(1, M):
        ct[k].wait_recv()
        back2_own(down[k])

    g2_add(1)
    g2_send(2)

    def back1(b):
        def step(t, _):
            at = pl.multiple_of(t * TL, TL)
            dh = dot(W2[b, :, 0:K], A[NA, :, pl.ds(at, TL)])
            for n in range(1, NA):
                dh = dh + dot(W2[b, :, n * K : (n + 1) * K], A[NA + n, :, pl.ds(at, TL)])
            norm = B[pl.ds(pl.multiple_of(b * LP, LP), U), pl.ds(pl.multiple_of(m * Q + t * TL, TL), TL)].astype(F32)
            grad = dh * col[b, :U, 24:25] + norm * col[b, :U, 25:26] + col[b, :U, 26:27]
            grad = (grad * H[b, :, pl.ds(at, TL)].astype(F32)).astype(BF16)
            H[b, :, pl.ds(at, TL)] = grad
            acc[0, :U] += lane_part(grad.astype(F32))
            return 0

        lax.fori_loop(0, NT, step, 0)
        ar4[d, pl.ds(b, 1), :] = row_of(0)
        acc[0:1] = jnp.zeros((1, LP, 128), F32)

        def mm(t, _):
            F[b, :, pl.ds(pl.multiple_of(t * LP, LP), LP)] = dot_nt(
                H[b], E1[:, pl.ds(pl.multiple_of(t * Q, Q), Q)]
            ).astype(BF16)
            return 0

        lax.fori_loop(0, PER, mm, 0)

    acc[0:1] = jnp.zeros((1, LP, 128), F32)
    ar4[d] = jnp.zeros((ar4.shape[1], LP), F32)
    K2 = 4 * K8
    FROM = {0: 0, 1: K2, 2: K2 + 2 * K8}
    order = [up[(j + 1) % M] for j in range(M)]
    def g1_cp(n, j):
        b = lax.rem(m + 1 + j, M)
        if n == 3:
            return remote(
                lanes(F.at[b], p * K8, K8), C.at[m, :, pl.ds(K - K8, K8)], g1s.at[3, j + 1], g1r.at[3, j + 1], (d, b)
            )
        return remote(
            lanes(F.at[b], HALF[n] * K8, K2 >> n), lanes(C.at[b], FROM[n], K2 >> n), g1s.at[n, j], g1r.at[n, j], PARTNER[n]
        )

    def g1_groups(b, j):
        mine = pl.ds(pl.multiple_of(p * K8, 128), K8)
        cps = []
        for k in range(1, G):
            to = (lax.rem(d + 8 * k, D), m)
            cps.append(send(lanes(F.at[b], p * K8, K8), x1.at[d // 8, j], x1s.at[k, j], x1r.at[k, j], to))
        x1[d // 8, j] = F[b, :, mine]
        for cp in cps:
            cp.wait_recv()
        for cp in cps:
            gone(cp)
        v = x1[0, j].astype(F32)
        for k in range(1, G):
            v = v + x1[k, j].astype(F32)
        F[b, :, mine] = v.astype(BF16)

    def g1_stage(n, j):
        b = lax.rem(m + 1 + j, M)
        g1_cp(n - 1, j).wait_recv()
        keep = pl.ds(pl.multiple_of(KEEP[n - 1] * K8, 128), K2 >> (n - 1))
        came = C[b, :, FROM[n - 1] : FROM[n - 1] + (K2 >> (n - 1))]
        F[b, :, keep] = (F[b, :, keep].astype(F32) + came.astype(F32)).astype(BF16)
        if n == 3 and G > 1:
            g1_groups(b, j)
        if n < 3 or not isinstance(j, int) or j < M - 1:
            g1_cp(n, j).start()
        else:
            C[m, :, K - K8 : K] = F[m, :, pl.ds(pl.multiple_of(p * K8, 128), K8)]

    def block(j, _):
        back1(lax.rem(m + 1 + j, M))
        g1_cp(0, j).start()
        for n in (3, 2, 1):
            pl.when(j >= n)(functools.partial(g1_stage, n, j - n))

        @pl.when(j == 1)
        def _():
            g2_add(2)
            g2_z()

        pl.when(j == 2)(functools.partial(g2_gather, 4))
        pl.when(j == 3)(functools.partial(g2_gather, 5))
        return 0

    lax.fori_loop(0, M, block, 0)
    cps4 = all_dp(ar4, a4s, a4r)
    for n in (3, 2, 1):
        g1_stage(n, M - n)
    g2_gather(6)

    def finish(t, _):
        at = pl.multiple_of(t * TL, TL)
        a = act2[:, pl.ds(at, TL)].astype(F32)
        act2[:, pl.ds(at, TL)] = (a * col[m, :U, 19:20] + col[m, :U, 20:21]).astype(BF16)
        return 0

    lax.fori_loop(0, M * NT, finish, 0)
    out_copy = pltpu.make_async_copy(act2, out_ref, loc.at[0])
    out_copy.start()
    tot4 = total(ar4, cps4)
    for b in range(M):
        ar4s[b] = jnp.broadcast_to(tot4[b : b + 1], (8, LP))
    ar4z[m] = ar4s[m]
    cps4z = [send(ar4s.at[up[k]], ar4z.at[m], a4zs.at[k], a4zr.at[k], (d, up[k])) for k in range(1, M)]
    g1_stage(3, M - 2)
    g1_stage(2, M - 1)
    g1_stage(3, M - 1)
    for b in range(M):
        g2cp[6, b].wait_recv()
    for b in range(M):
        slo2[:, b * U : (b + 1) * U] = B[b * LP : b * LP + U, pl.ds(L2, LP)][:, :U]
    gw2_copy = pltpu.make_async_copy(lanes(slo2, 0, gw2_ref.shape[1]), gw2_ref, loc.at[2])
    gw2_copy.start()
    for j in range(M - 1):
        g1_cp(3, j).wait_recv()
    v = C[0, :, K - K8 : K].astype(F32)
    for b in range(1, M):
        v = v + C[b, :, K - K8 : K].astype(F32)
    G1[:, pl.ds(pl.multiple_of(p * K8, 128), K8)] = v.astype(BF16)
    ga = send(lanes(G1, p * K8, K8), lanes(G1, p * K8, K8), g1s.at[4, 0], g1r.at[4, 0], lo_dev)
    ga.wait_recv()
    part = lanes(G1, (4 * c + 2 * hi) * K8, 2 * K8)
    ga = send(part, part, g1s.at[4, 1], g1r.at[4, 1], hi_dev)
    ga.wait_recv()
    part = lanes(G1, 4 * c * K8, K2)
    ga = send(part, part, g1s.at[4, 2], g1r.at[4, 2], core_dev)
    for cp in cps4z:
        cp.wait_recv()
    v = ar4z[0]
    for b in range(1, M):
        v = v + ar4z[b]
    vec_ref[0:1, :] = v[0:1]
    ga.wait_recv()
    gw1_copy = pltpu.make_async_copy(lanes(G1, 0, K), gw1_ref, loc.at[1])
    gw1_copy.start()
    for cp in [*ag2.values(), *g2cp.values(), *(g1_cp(n, j) for n in range(4) for j in range(M - n // 3))]:
        cp.wait_send()
    out_copy.wait()
    gw1_copy.wait()
    gw2_copy.wait()
    for cp in sent:
        cp.wait_send()


def per_device(ids, hash_mult, hash_add, w1, b1, s1, t1, w2, b2, s2, t2, cot):
    D, M = lax.axis_size("dp"), lax.axis_size("mp")
    U, K = w1.shape
    R = ids.shape[0]
    Q = R // M
    LP = -(-U // 128) * 128
    G = D // 8
    par = jnp.pad(jnp.stack([b1, s1, t1, b2, s2, t2]), ((0, 2), (0, LP - U)))
    dma = pltpu.SemaphoreType.DMA
    vmem = pl.BlockSpec(memory_space=pltpu.VMEM)
    hbm = pl.BlockSpec(memory_space=pl.ANY)
    AR = -(-2 * M // 8) * 8
    scratch = [
        pltpu.VMEM((M, K, Q), BF16),
        pltpu.VMEM((M * LP, R), BF16),
        pltpu.VMEM((M, U, max(K, Q)), BF16),
        pltpu.VMEM((M, U, M * LP), BF16),
        pltpu.VMEM((U, max(K, M * U)), BF16),
        pltpu.VMEM((LP, M * LP), BF16),
        pltpu.VMEM((M, U, max(K, Q)), BF16),
        pltpu.VMEM((M, U, Q), BF16),
        pltpu.VMEM((U, R), BF16),
        pltpu.VMEM((U, R), BF16),
        pltpu.VMEM((M, LP, 128), F32),
        pltpu.VMEM((M, 32, LP), F32),
        pltpu.VMEM((4, LP, 128), F32),
        pltpu.VMEM((K, 128), F32),
        pltpu.VMEM((M, 8, LP), F32),
        pltpu.VMEM((D, AR, LP), F32),
        pltpu.VMEM((D, 8, LP), F32),
        pltpu.VMEM((M, 8, LP), F32),
        pltpu.VMEM((D, AR + 8, LP), F32),
        pltpu.VMEM((M, AR, LP), F32),
        pltpu.VMEM((D, 8, LP), F32),
        pltpu.VMEM((M, 8, LP), F32),
        pltpu.VMEM((M, 8, LP), F32),
        dma((4, M)), dma((4, M)), dma((4, M)), dma((4, M)),
        dma((M,)), dma((M,)), dma((M,)), dma((M,)), dma((3 + M,)),
        dma((D,)), dma((D,)), dma((D,)), dma((D,)), dma((M,)), dma((M,)),
        dma((D,)), dma((D,)), dma((M,)), dma((M,)), dma((D,)), dma((D,)), dma((M,)), dma((M,)),
        dma((5, M)), dma((5, M)), dma((7, M)), dma((7, M)), pltpu.SemaphoreType.REGULAR((2 + M,)),
    ]
    if G > 1:
        scratch += [
            pltpu.VMEM((G, M, U, K // 8), BF16),
            pltpu.VMEM((G, M, LP // 8, LP), BF16),
            dma((G, M)), dma((G, M)), dma((G, M)), dma((G, M)),
        ]
    out, gw1, gw2, vec = pl.pallas_call(
        functools.partial(kernel, D, M, U, LP, K, R),
        out_shape=[
            jax.ShapeDtypeStruct((U, R), BF16),
            jax.ShapeDtypeStruct((U, K), BF16),
            jax.ShapeDtypeStruct((U, -(-M * U // 128) * 128), BF16),
            jax.ShapeDtypeStruct((8, LP), F32),
        ],
        in_specs=[vmem] * 4 + [hbm, hbm, hbm],
        out_specs=[hbm, hbm, hbm, vmem],
        scratch_shapes=scratch,
        compiler_params=pltpu.CompilerParams(
            collective_id=0, has_side_effects=True, vmem_limit_bytes=64 * 2**20 - 2**16
        ),
    )(ids[None, :], hash_mult[None, :], hash_add[None, :], par, w1, w2, cot)
    v = vec[:, :U]
    return (out, gw1.astype(F32), v[0], v[1], v[2], gw2[:, : M * U].astype(F32), v[3], v[4], v[5])


def solution(mesh):
    return jax.shard_map(
        per_device,
        mesh=mesh,
        in_specs=(
            P("dp"), P(), P(), P("mp", None), P("mp"), P("mp"), P("mp"),
            P("mp", None), P("mp"), P("mp"), P("mp"), P("mp", "dp"),
        ),
        out_specs=(
            P("mp", "dp"), P("mp", None), P("mp"), P("mp"), P("mp"),
            P("mp", None), P("mp"), P("mp"), P("mp"),
        ),
        check_vma=False,
    )
```

profile of v0, /device:TPU:9, one launch (start us, length us, event | category | flops | bytes accessed | tf_op | source)
XLA Modules:
  0.0 195.1 jit_solution(14064761571559474003)
XLA Ops:
  0.6 0.8 stack.27
  1.4 0.6 pad.4.par_ref
  2.0 184.5 %shard_map.187 = (bf16[450,4096]{1,0:T(8,128)(2,1)}, bf16[450,1024]{1,0:T(8,128)(2,1)}, bf16[450,1920]{1,0:T(8,128)(2,1)}, f32[8,512]{1,0:T(8,128)}) custom-call(s32[1,4096]{1,0:T(1,128)} %bitcast.15, s32[1,1024]{1,0:T(1,128)} %bitcast.16, s32[1,1024]{1,0:T(1,128)} %bitcast.17, f32[8,512]{1,0:T(8,128)} %pad.4.par_ref, bf16[450,1024]{1,0:T(8,128)(2,1)} %w1_ref.1, ...), custom_call_target="tpu_custom_call" | custom-call | tf_op jit(solution)/shard_map/pallas_call | solution.py:788
  186.6 0.0 copy-start.1
  186.6 1.5 fusion
  188.1 0.0 copy-start
  188.1 3.6 %slice_convert_fusion = f32[450,1800]{1,0:T(8,128)} fusion(bf16[450,1920]{1,0:T(8,128)(2,1)} %get-tuple-element.16), kind=kLoop, calls=%fused_computation | loop fusion | flops 810000 | bytes 4860000 | tf_op jit(solution)/shard_map/convert_element_type | solution.py:804
  191.8 0.0 copy-done.1
  191.8 1.5 convert_element_type.8
  193.2 0.0 copy-done
  193.2 1.9 copy.22
Async XLA Ops:
  186.6 5.2 %copy-start.1 = (bf16[450,1024]{1,0:T(8,128)(2,1)S(1)}, bf16[450,1024]{1,0:T(8,128)(2,1)}, u32[]{:S(2)}) copy-start(bf16[450,1024]{1,0:T(8,128)(2,1)} %get-tuple-element.14) | copy-start | bytes 2764804
  188.1 5.1 %copy-start = (bf16[450,4096]{1,0:T(8,128)(2,1)S(1)}, bf16[450,4096]{1,0:T(8,128)(2,1)}, u32[]{:S(2)}) copy-start(bf16[450,4096]{1,0:T(8,128)(2,1)} %get-tuple-element.32) | copy-start | bytes 11059204
where the time goes:
time: 195 us
  Pallas kernels  185 us (95%)
  other arithmetic  5.08 us (3%)
  local copies, waits for them, and re-layouts  4.81 us (2%)
    pallas_call x1, Pallas kernels, per_device(): pl.pallas_call(functools.partial(kernel, D, M, U, LP, K, R), out_shape=[j...  185 us

commit v1 on v0

--- a/solution.py
+++ b/solution.py
@@ -46,7 +46,7 @@
 
 def kernel(
     D, M, U, LP, K, R,
-    ids_ref, mult_ref, add_ref, par_ref, w1_ref, w2_ref, cot_ref,
+    ids_ref, mult_ref, add_ref, b1_ref, s1_ref, t1_ref, b2_ref, s2_ref, t2_ref, w1_ref, w2_ref, cot_ref,
     out_ref, gw1_ref, gw2_ref, vec_ref,
     A, B, C, W2, G1, E1, F, H, act2, slo2, col, RW, acc, hcol,
     pv, ar1, ar2, ar2z, ar3, ar3z, ar4, ar4s, ar4z,
@@ -116,12 +116,14 @@
     w1_loc = pltpu.make_async_copy(w1_ref, C.at[m], loc.at[0])
     w1_loc.start()
     cot_loc = pltpu.make_async_copy(lanes(cot_ref, m * Q, Q), lanes(F.at[m], 0, Q), loc.at[2])
-    pv[m] = par_ref[...]
+    pv[m] = jnp.zeros((8, LP), F32)
+    for n, ref in enumerate((b1_ref, s1_ref, t1_ref, b2_ref, s2_ref, t2_ref)):
+        pv[m, n : n + 1, :U] = ref[...]
     pl.semaphore_wait(bar, len(greeted))
 
     ag1, ag2, agp, ct = {}, {}, {}, {}
     for k in range(1, M):
-        agp[k] = send(par_ref, pv.at[m], pvs.at[k], pvr.at[k], (d, up[k]))
+        agp[k] = send(pv.at[m], pv.at[m], pvs.at[k], pvr.at[k], (d, up[k]))
     for ag, own, buf, size, ss, rs in ((ag1, w1_ref, C, K8, w1s, w1r), (ag2, None, W2, J8, w2s, w2r)):
         for k in range(1, M):
             part = lanes(buf.at[m], p * size, size)
@@ -198,7 +200,7 @@
         B[pl.ds(b * LP + U // 16 * 16, LP - U // 16 * 16), :] = jnp.zeros((LP - U // 16 * 16, R), BF16)
 
     RW[...] = jnp.zeros_like(RW)
-    RW[m, 0:8] = par_ref[...]
+    RW[m, 0:8] = pv[m]
     make_col(m)
     encode(m, to_a(m))
     w1_loc.wait()
@@ -737,6 +739,36 @@
         cp.wait_send()
 
 
+def finish(U, out_in, gw1_in, gw2_in, vec_in, out_ref, gw1_ref, gw2_ref, *tail):
+    *vecs, held, held1, held2, wide1, wide2, sem_in, sem_out = tail
+    n = 4
+    width = held.shape[1] // n
+    pieces = [pl.ds(k * width, width) for k in range(n)]
+    ins = [
+        pltpu.make_async_copy(gw2_in, held2, sem_in.at[n]),
+        pltpu.make_async_copy(gw1_in, held1, sem_in.at[n + 1]),
+    ] + [pltpu.make_async_copy(out_in.at[:, at], held.at[:, at], sem_in.at[k]) for k, at in enumerate(pieces)]
+    for cp in ins:
+        cp.start()
+    outs = [
+        pltpu.make_async_copy(wide2, gw2_ref, sem_out.at[n]),
+        pltpu.make_async_copy(wide1, gw1_ref, sem_out.at[n + 1]),
+    ] + [pltpu.make_async_copy(held.at[:, at], out_ref.at[:, at], sem_out.at[k]) for k, at in enumerate(pieces)]
+    ins[0].wait()
+    wide2[...] = held2[:, : wide2.shape[1]].astype(F32)
+    outs[0].start()
+    ins[1].wait()
+    wide1[...] = held1[...].astype(F32)
+    outs[1].start()
+    for k in range(n):
+        ins[2 + k].wait()
+        outs[2 + k].start()
+    for k, ref in enumerate(vecs):
+        ref[...] = vec_in[k : k + 1, :U]
+    for cp in outs:
+        cp.wait()
+
+
 def per_device(ids, hash_mult, hash_add, w1, b1, s1, t1, w2, b2, s2, t2, cot):
     D, M = lax.axis_size("dp"), lax.axis_size("mp")
     U, K = w1.shape
@@ -744,7 +776,7 @@
     Q = R // M
     LP = -(-U // 128) * 128
     G = D // 8
-    par = jnp.pad(jnp.stack([b1, s1, t1, b2, s2, t2]), ((0, 2), (0, LP - U)))
+    par = [x[None, :] for x in (b1, s1, t1, b2, s2, t2)]
     dma = pltpu.SemaphoreType.DMA
     vmem = pl.BlockSpec(memory_space=pltpu.VMEM)
     hbm = pl.BlockSpec(memory_space=pl.ANY)
@@ -793,15 +825,36 @@
             jax.ShapeDtypeStruct((U, -(-M * U // 128) * 128), BF16),
             jax.ShapeDtypeStruct((8, LP), F32),
         ],
-        in_specs=[vmem] * 4 + [hbm, hbm, hbm],
+        in_specs=[vmem] * 9 + [hbm, hbm, hbm],
         out_specs=[hbm, hbm, hbm, vmem],
         scratch_shapes=scratch,
         compiler_params=pltpu.CompilerParams(
             collective_id=0, has_side_effects=True, vmem_limit_bytes=64 * 2**20 - 2**16
         ),
-    )(ids[None, :], hash_mult[None, :], hash_add[None, :], par, w1, w2, cot)
-    v = vec[:, :U]
-    return (out, gw1.astype(F32), v[0], v[1], v[2], gw2[:, : M * U].astype(F32), v[3], v[4], v[5])
+    )(ids[None, :], hash_mult[None, :], hash_add[None, :], *par, w1, w2, cot)
+    out, gw1, gw2, *v = pl.pallas_call(
+        functools.partial(finish, U),
+        out_shape=[
+            jax.ShapeDtypeStruct((U, R), BF16),
+            jax.ShapeDtypeStruct((U, K), F32),
+            jax.ShapeDtypeStruct((U, M * U), F32),
+        ]
+        + [jax.ShapeDtypeStruct((1, U), F32)] * 6,
+        in_specs=[hbm, hbm, hbm, vmem],
+        out_specs=[hbm, hbm, hbm] + [vmem] * 6,
+        scratch_shapes=[
+            pltpu.VMEM((U, R), BF16),
+            pltpu.VMEM((U, K), BF16),
+            pltpu.VMEM(gw2.shape, BF16),
+            pltpu.VMEM((U, K), F32),
+            pltpu.VMEM((U, M * U), F32),
+            dma((6,)),
+            dma((6,)),
+        ],
+        compiler_params=pltpu.CompilerParams(vmem_limit_bytes=63 * 2**20),
+    )(out, gw1, gw2, vec)
+    v = [x[0] for x in v]
+    return (out, gw1, v[0], v[1], v[2], gw2, v[3], v[4], v[5])
 
 
 def solution(mesh):

time: 195 us -> 192 us (0.985)
  Pallas kernels: 185 us -> 191 us
  other arithmetic: 5.08 us -> 0 us
  local copies, waits for them, and re-layouts: 4.81 us -> 0 us
    pallas_call x0 -> x1, Pallas kernels: none -> 6.66 us  [per_device(): pl.pallas_call(functools.partial(finish, U), out_shape=[jax.ShapeDtypeStr...]
    convert_element_type x2 -> x0, other arithmetic: 5.08 us -> none  [the longest x1 3.63 us: per_device(): gw2[:, :M * U].astype(F32)]
where the time goes in v1:
time: 192 us
  Pallas kernels  191 us (99%)
    pallas_call x1, Pallas kernels, per_device(): pl.pallas_call(functools.partial(kernel, D, M, U, LP, K, R), out_shape=[j...  185 us
    pallas_call x1, Pallas kernels, per_device(): pl.pallas_call(functools.partial(finish, U), out_shape=[jax.ShapeDtypeStr...  6.66 us

profile of v1, /device:TPU:9, one launch (start us, length us, event | category | flops | bytes accessed | tf_op | source)
XLA Modules:
  0.0 192.1 jit_solution(11120690400207767919)
XLA Ops:
  0.6 184.6 %shard_map.187 = (bf16[450,4096]{1,0:T(8,128)(2,1)}, bf16[450,1024]{1,0:T(8,128)(2,1)}, bf16[450,1920]{1,0:T(8,128)(2,1)}, f32[8,512]{1,0:T(8,128)}) custom-call(s32[1,4096]{1,0:T(1,128)} %bitcast.15, s32[1,1024]{1,0:T(1,128)} %bitcast.16, s32[1,1024]{1,0:T(1,128)} %bitcast.17, f32[1,450]{1,0:T(1,128)} %bitcast.18, f32[1,450]{1,0:T(1,128)} %bitcast.19, ...), custom_call_target="tpu_custom_call" | custom-call | tf_op jit(solution)/shard_map/pallas_call | solution.py:820
  185.3 6.7 %shard_map.188 = (bf16[450,4096]{1,0:T(8,128)(2,1)}, f32[450,1024]{1,0:T(8,128)}, f32[450,1800]{1,0:T(8,128)}, f32[1,450]{1,0:T(1,128)}, f32[1,450]{1,0:T(1,128)...) custom-call(bf16[450,4096]{1,0:T(8,128)(2,1)} %get-tuple-element.22.out_in, ...), custom_call_target="tpu_custom_call" | custom-call | tf_op jit(solution)/shard_map/pallas_call | solution.py:835

commit v2 on v1

--- a/solution.py
+++ b/solution.py
@@ -592,8 +592,6 @@
         ct[k].wait_recv()
         back2_own(down[k])
 
-    g2_add(1)
-    g2_send(2)
 
     def back1(b):
         def step(t, _):
@@ -670,6 +668,11 @@
         for n in (3, 2, 1):
             pl.when(j >= n)(functools.partial(g1_stage, n, j - n))
 
+        @pl.when(j == 0)
+        def _():
+            g2_add(1)
+            g2_send(2)
+
         @pl.when(j == 1)
         def _():
             g2_add(2)
@@ -714,13 +717,13 @@
     for b in range(1, M):
         v = v + C[b, :, K - K8 : K].astype(F32)
     G1[:, pl.ds(pl.multiple_of(p * K8, 128), K8)] = v.astype(BF16)
-    ga = send(lanes(G1, p * K8, K8), lanes(G1, p * K8, K8), g1s.at[4, 0], g1r.at[4, 0], lo_dev)
-    ga.wait_recv()
-    part = lanes(G1, (4 * c + 2 * hi) * K8, 2 * K8)
-    ga = send(part, part, g1s.at[4, 1], g1r.at[4, 1], hi_dev)
-    ga.wait_recv()
+    diag_dev = (d + 2 - 4 * x + 4 - 8 * y, m)
+    mine = lanes(G1, p * K8, K8)
+    ga = [send(mine, mine, g1s.at[4, n], g1r.at[4, n], dev) for n, dev in enumerate((diag_dev, hi_dev, lo_dev))]
+    for cp in ga:
+        cp.wait_recv()
     part = lanes(G1, 4 * c * K8, K2)
-    ga = send(part, part, g1s.at[4, 2], g1r.at[4, 2], core_dev)
+    ga = send(part, part, g1s.at[4, 3], g1r.at[4, 3], core_dev)
     for cp in cps4z:
         cp.wait_recv()
     v = ar4z[0]

time: 192 us -> 188 us (0.979)
  Pallas kernels: 191 us -> 187 us
    pallas_call x1, Pallas kernels: 185 us -> 180 us  [per_device(): pl.pallas_call(functools.partial(kernel, D, M, U, LP, K, R), out_shape=[j...]
where the time goes in v2:
time: 188 us
  Pallas kernels  187 us (99%)
    pallas_call x1, Pallas kernels, per_device(): pl.pallas_call(functools.partial(kernel, D, M, U, LP, K, R), out_shape=[j...  180 us
    pallas_call x1, Pallas kernels, per_device(): pl.pallas_call(functools.partial(finish, U), out_shape=[jax.ShapeDtypeStr...  6.66 us

profile of v2, /device:TPU:9, one launch (start us, length us, event | category | flops | bytes accessed | tf_op | source)
XLA Modules:
  0.0 187.6 jit_solution(2650301072076080904)
XLA Ops:
  0.6 180.1 %shard_map.187 = (bf16[450,4096]{1,0:T(8,128)(2,1)}, bf16[450,1024]{1,0:T(8,128)(2,1)}, bf16[450,1920]{1,0:T(8,128)(2,1)}, f32[8,512]{1,0:T(8,128)}) custom-call(s32[1,4096]{1,0:T(1,128)} %bitcast.15, s32[1,1024]{1,0:T(1,128)} %bitcast.16, s32[1,1024]{1,0:T(1,128)} %bitcast.17, f32[1,450]{1,0:T(1,128)} %bitcast.18, f32[1,450]{1,0:T(1,128)} %bitcast.19, ...), custom_call_target="tpu_custom_call" | custom-call | tf_op jit(solution)/shard_map/pallas_call | solution.py:823
  180.8 6.7 %shard_map.188 = (bf16[450,4096]{1,0:T(8,128)(2,1)}, f32[450,1024]{1,0:T(8,128)}, f32[450,1800]{1,0:T(8,128)}, f32[1,450]{1,0:T(1,128)}, f32[1,450]{1,0:T(1,128)...) custom-call(bf16[450,4096]{1,0:T(8,128)(2,1)} %get-tuple-element.22.out_in, ...), custom_call_target="tpu_custom_call" | custom-call | tf_op jit(solution)/shard_map/pallas_call | solution.py:838

commit v3 on v2

--- a/solution.py
+++ b/solution.py
@@ -688,6 +688,13 @@
         g1_stage(n, M - n)
     g2_gather(6)
 
+    tot4 = total(ar4, cps4)
+    for b in range(M):
+        ar4s[b] = jnp.broadcast_to(tot4[b : b + 1], (8, LP))
+    ar4z[m] = ar4s[m]
+    cps4z = [send(ar4s.at[up[k]], ar4z.at[m], a4zs.at[k], a4zr.at[k], (d, up[k])) for k in range(1, M)]
+    g1_stage(3, M - 2)
+    g1_stage(2, M - 1)
     def finish(t, _):
         at = pl.multiple_of(t * TL, TL)
         a = act2[:, pl.ds(at, TL)].astype(F32)
@@ -697,13 +704,6 @@
     lax.fori_loop(0, M * NT, finish, 0)
     out_copy = pltpu.make_async_copy(act2, out_ref, loc.at[0])
     out_copy.start()
-    tot4 = total(ar4, cps4)
-    for b in range(M):
-        ar4s[b] = jnp.broadcast_to(tot4[b : b + 1], (8, LP))
-    ar4z[m] = ar4s[m]
-    cps4z = [send(ar4s.at[up[k]], ar4z.at[m], a4zs.at[k], a4zr.at[k], (d, up[k])) for k in range(1, M)]
-    g1_stage(3, M - 2)
-    g1_stage(2, M - 1)
     g1_stage(3, M - 1)
     for b in range(M):
         g2cp[6, b].wait_recv()

time: 188 us -> 188 us (level)
  no operation moved by 1% of the time
where the time goes in v3:
time: 188 us
  Pallas kernels  187 us (99%)
    pallas_call x1, Pallas kernels, per_device(): pl.pallas_call(functools.partial(kernel, D, M, U, LP, K, R), out_shape=[j...  180 us
    pallas_call x1, Pallas kernels, per_device(): pl.pallas_call(functools.partial(finish, U), out_shape=[jax.ShapeDtypeStr...  6.66 us

profile of v3, /device:TPU:9, one launch (start us, length us, event | category | flops | bytes accessed | tf_op | source)
XLA Modules:
  0.0 187.6 jit_solution(6574441890105003689)
XLA Ops:
  0.6 180.1 %shard_map.187 = (bf16[450,4096]{1,0:T(8,128)(2,1)}, bf16[450,1024]{1,0:T(8,128)(2,1)}, bf16[450,1920]{1,0:T(8,128)(2,1)}, f32[8,512]{1,0:T(8,128)}) custom-call(s32[1,4096]{1,0:T(1,128)} %bitcast.15, s32[1,1024]{1,0:T(1,128)} %bitcast.16, s32[1,1024]{1,0:T(1,128)} %bitcast.17, f32[1,450]{1,0:T(1,128)} %bitcast.18, f32[1,450]{1,0:T(1,128)} %bitcast.19, ...), custom_call_target="tpu_custom_call" | custom-call | tf_op jit(solution)/shard_map/pallas_call | solution.py:823
  180.8 6.7 %shard_map.188 = (bf16[450,4096]{1,0:T(8,128)(2,1)}, f32[450,1024]{1,0:T(8,128)}, f32[450,1800]{1,0:T(8,128)}, f32[1,450]{1,0:T(1,128)}, f32[1,450]{1,0:T(1,128)...) custom-call(bf16[450,4096]{1,0:T(8,128)(2,1)} %get-tuple-element.22.out_in, ...), custom_call_target="tpu_custom_call" | custom-call | tf_op jit(solution)/shard_map/pallas_call | solution.py:838
